TPU v7x, 128 devices: a whole 4x4x4 slice. The times are simulated.
128 devices in a mesh: row: 8 (over x, core), col: 16 (over z, y).
Axes of the slice: x: 4, y: 4, z: 4, core: 2. Of those that a mesh axis runs over, the one named last changes fastest.
Arguments:
- amplitudes: bfloat16 [1792, 23040], P('col', 'row'), may hold values from -6 to 6
- integrals: bfloat16 [23040, 23040], P('row', 'col'), may hold values from -0.026352314 to 0.026352314, as said below
- row_gap: float32 [1792], replicated, may hold values from 0.25 to 1
- col_gap: float32 [23040], replicated, may hold values from 0.25 to 1
Outputs:
- updated: bfloat16 [1792, 23040], P(None, ('row', 'col'))
Inputs may be any that keep to these rules, and one draw needn't show every extreme that they name: integrals is symmetric: entry (p, q) equals entry (q, p).
All inputs are finite; a program needn't handle non-finite values.
Results may differ from a plain program's by a relative error of at most 0.022.
Values may be sent and summed in bfloat16 or wider, within the bound.
A program may use at most 64 MiB of HBM per device.

v0:
```python
import functools

import jax
import jax.numpy as jnp
from jax import lax
from jax.experimental import pallas as pl
from jax.experimental.pallas import tpu as pltpu
from jax.sharding import PartitionSpec as P

MESH = pl.DeviceIdType.MESH
F32 = jnp.float32
BF16 = jnp.bfloat16

BLOCK = 16
WINDOW = 192
STRIDE = 176
TILE = 128
CUT = 368
SLOTS = 4
X_KIND = 14
RS_KIND = 24
KINDS = 40

PLAN = (
    ("r1", 8),
    ("r2", 10),
    ("a0", 0),
    ("cw", 7),
    ("m1", 3),
    ("b2", 4),
    ("b4", 5),
    ("r3", 12),
    ("a3", 2),
    ("a2", 1),
    ("r4", 14),
    ("sw", 14),
    ("tv", 0),
    ("gp", 3),
    ("a1", 0),
    ("rw", 10),
    ("m2", 6),
    ("gw", 7),
    ("b1", 3),
    ("b3", 4),
    ("b5", 5),
)


def kernel(
    a_ref, vt_hbm, row_ref, col_ref, o_ref,
    near, cg, cf, rc, v, vt, vtail, turned, ag, tg, c1, cx, xo, xn, sg, wq, w1, w2, ro1, rn1, ro2, rn2, out, lsem, tsend, trecv, send, recv,
):
    chunks = ag.shape[0]
    depth, width = a_ref.shape[1], v.shape[1]
    group, final = depth // 4, o_ref.shape[0]
    row, col = lax.axis_index("row"), lax.axis_index("col")
    x, core = row // 2, row % 2
    z, y = col // 4, col % 4
    half = core * 128
    other = 128 - half

    def around(index):
        return {0: index, 1: lax.rem(index + 1, 4), 2: lax.rem(index + 2, 4), -1: lax.rem(index + 3, 4)}

    xs, ys, zs = around(x), around(y), around(z)
    at = {"z": zs, "y": ys}
    peer = {
        ("x", 1): (xs[1] * 2 + core, col),
        ("x", -1): (xs[-1] * 2 + core, col),
        ("y", 1): (row, z * 4 + ys[1]),
        ("y", -1): (row, z * 4 + ys[-1]),
        ("z", 1): (row, zs[1] * 4 + y),
        ("z", -1): (row, zs[-1] * 4 + y),
        "core": (x * 2 + 1 - core, col),
    }
    strips = {step: half + index * 32 for step, index in xs.items()}
    main = ag.shape[-1]
    gather = (("y", "z", pl.ds(0, main // 2)), ("z", "y", pl.ds(main // 2, main // 2)))
    scatter = (("z", "y"), ("y", "z"))

    barrier = pltpu.get_barrier_semaphore()
    for to in peer.values():
        pl.semaphore_signal(barrier, inc=1, device_id=to, device_id_type=MESH)

    def copy(c, kind, src, dst, to):
        return pltpu.make_async_remote_copy(
            src_ref=src, dst_ref=dst, send_sem=send.at[c, kind], recv_sem=recv.at[c, kind],
            device_id=to, device_id_type=MESH,
        )

    def arrived(c, kind, dst):
        copy(c, kind, dst, dst, peer["core"]).wait_recv()

    def sent(c, kind, src):
        copy(c, kind, src, src, peer["core"]).wait_send()

    def block(s, c, step):
        first, _, lanes = gather[s]
        f = at[first][step]
        return ag.at[c, z, f, :, lanes] if first == "y" else ag.at[c, f, y, :, lanes]

    def line(s, c, step, start=0, size=4):
        first, second, lanes = gather[s]
        g, part = at[second][step], pl.ds(start, size)
        return ag.at[c, g, part, :, lanes] if first == "y" else ag.at[c, part, g, :, lanes]

    def a_send(c, s, k, d=1):
        first, second, _ = gather[s]
        if k == 0:
            return block(s, c, 0), peer[first, 1]
        if k == 1:
            return block(s, c, 0), peer[first, -1]
        if k == 2:
            return block(s, c, -d), peer[first, d]
        if k == 3:
            return line(s, c, 0), peer[second, 1]
        if k == 4:
            return line(s, c, 0), peer[second, -1]
        if k == 5:
            return line(s, c, -1, 0, 2), peer[second, 1]
        return line(s, c, 1, 2, 2), peer[second, -1]

    def a_land(c, s, k):
        if k < 3:
            return block(s, c, (-1, 1, 2)[k])
        if k < 5:
            return line(s, c, (-1, 1)[k - 3])
        return line(s, c, 2, 2 * (k - 5), 2)

    def a_start(c, s, k, d=1):
        src, to = a_send(c, s, k, d)
        copy(c, s * 7 + k, src, src, to).start()

    def a_wait(c, s, k):
        arrived(c, s * 7 + k, a_land(c, s, k))

    def t_line(step, start=0, size=4):
        return tg.at[zs[step], pl.ds(start, size)]

    def t_send(k):
        return (
            (tg.at[z, y], peer["y", 1]),
            (tg.at[z, y], peer["y", -1]),
            (tg.at[z, ys[-1]], peer["y", 1]),
            (t_line(0), peer["z", 1]),
            (t_line(0), peer["z", -1]),
            (t_line(-1, 0, 2), peer["z", 1]),
            (t_line(1, 2, 2), peer["z", -1]),
        )[k]

    def t_land(k):
        return (
            tg.at[z, ys[-1]], tg.at[z, ys[1]], tg.at[z, ys[2]],
            t_line(-1), t_line(1), t_line(2, 0, 2), t_line(2, 2, 2),
        )[k]

    def t_copy(k, src, to):
        return pltpu.make_async_remote_copy(
            src_ref=src, dst_ref=src, send_sem=tsend.at[k], recv_sem=trecv.at[k], device_id=to, device_id_type=MESH
        )

    def t_start(*kinds):
        for k in kinds:
            t_copy(k, *t_send(k)).start()

    def t_wait(*kinds):
        for k in kinds:
            t_copy(k, t_land(k), peer["core"]).wait_recv()

    def a0(c):
        ag[c, z, y] = a_ref[pl.ds(pl.multiple_of(c * BLOCK, BLOCK), BLOCK), :main]
        for s in range(2):
            a_start(c, s, 0)
            a_start(c, s, 1)
        pl.when(c == 0)(lambda: t_start(0, 1))

    def a1(c):
        def forward(d):
            for s in range(2):
                a_wait(c, s, 0 if d == 1 else 1)
                a_start(c, s, 2, d)

        @pl.when(c == 0)
        def _():
            t_wait(0)
            t_start(2)

        pl.when(c % 2 == 0)(lambda: forward(1))
        pl.when(c % 2 == 1)(lambda: forward(-1))

    def a2(c):
        pl.when(c % 2 == 0)(lambda: [a_wait(c, s, 1) for s in range(2)] and None)
        pl.when(c % 2 == 1)(lambda: [a_wait(c, s, 0) for s in range(2)] and None)
        for s in range(2):
            a_wait(c, s, 2)
            a_start(c, s, 3)
            a_start(c, s, 4)

        @pl.when(c == 0)
        def _():
            t_wait(1, 2)
            t_start(3, 4)

    def a3(c):
        for s in range(2):
            a_wait(c, s, 3)
            a_start(c, s, 5)
            a_wait(c, s, 4)
            a_start(c, s, 6)

        @pl.when(c == 0)
        def _():
            t_wait(3)
            t_start(5)
            t_wait(4)
            t_start(6)

    def m1(c):
        for s in range(2):
            a_wait(c, s, 5)
            a_wait(c, s, 6)
        pl.when(c == 0)(lambda: t_wait(5, 6))
        ends = tg[:, :, pl.ds(pl.multiple_of(c // 2 * BLOCK, BLOCK), BLOCK), :].reshape(16 * BLOCK, 128)
        mine = lax.broadcasted_iota(jnp.int32, (16 * BLOCK, 128), 1) // 64 == c % 2
        ends = jnp.where(mine, ends.astype(F32), 0.0).astype(BF16)
        rows = ag[c].reshape(16 * BLOCK, main)
        middle = (width // 2 + 127) // 128 * 128
        last = (((1,), (1,)), ((), ()))
        for lo, hi in ((0, middle), (middle, width)):
            part = lax.dot_general(vt[lo:hi, :main], rows, last, preferred_element_type=F32)
            part = part + lax.dot_general(vtail[lo:hi], ends, last, preferred_element_type=F32)
            c1[c % SLOTS, :, lo:hi] = part.astype(BF16).T
        x_start(c, 0)

    def piece(step, start=0, size=32):
        return pl.ds(pl.multiple_of(strips[step] + start, 16), size)

    def x_send(c, k):
        if k == 0:
            return c1.at[c % SLOTS, pl.ds(pl.multiple_of(other, 128), 128)], cx.at[c % SLOTS], peer["core"]
        if k == 9:
            src = sg.at[c % SLOTS, pl.ds(pl.multiple_of(half, 128), 128)]
            return src, src, peer["core"]
        d = 1 if k % 2 == 1 else -1
        part = pl.ds(8 - 8 * d, 16)
        if k < 3:
            return c1.at[c % SLOTS, piece(2, 8 - 8 * d, 16)], xo.at[c, part], peer["x", d]
        if k < 5:
            return c1.at[c % SLOTS, piece(d)], xn.at[c, (k - 3)], peer["x", d]
        src = sg.at[c % SLOTS, piece(0) if k < 7 else piece(-d, 8 - 8 * d, 16)]
        return src, src, peer["x", d]

    def x_land(c, k):
        if k < 5:
            return x_send(c, k)[1]
        if k == 9:
            return sg.at[c % SLOTS, pl.ds(pl.multiple_of(other, 128), 128)]
        d = 1 if k % 2 == 1 else -1
        return sg.at[c % SLOTS, piece(-d) if k < 7 else piece(2, 8 - 8 * d, 16)]

    def x_start(c, k):
        src, dst, to = x_send(c, k)
        copy(c, X_KIND + k, src, dst, to).start()

    def x_wait(c, k):
        arrived(c, X_KIND + k, x_land(c, k))

    def b1(c):
        x_wait(c, 0)
        rows = pl.ds(pl.multiple_of(half, 128), 128)
        c1[c % SLOTS, rows, :] = (c1[c % SLOTS, rows, :].astype(F32) + cx[c % SLOTS].astype(F32)).astype(BF16)
        x_start(c, 1)
        x_start(c, 2)

    def b2(c):
        for k, step in ((1, 1), (2, -1)):
            x_wait(c, k)
            part, rows = pl.ds(16 * (k - 1), 16), piece(step, 16 * (k - 1), 16)
            c1[c % SLOTS, rows, :] = (c1[c % SLOTS, rows, :].astype(F32) + xo[c, part].astype(F32)).astype(BF16)
            x_start(c, k + 2)

    def b3(c):
        gap = rc[pl.ds(core * 8 + x * 2, 2), c].reshape(32, 128)
        x_wait(c, 3)
        x_wait(c, 4)
        rows = piece(0)
        total = c1[c % SLOTS, rows, :].astype(F32) + xn[c, 0].astype(F32) + xn[c, 1].astype(F32)
        sg[c % SLOTS, rows, :] = (total / (gap[:, :1] + cg[0:1, :width])).astype(BF16)
        x_start(c, 5)
        x_start(c, 6)

    def b4(c):
        for k in (5, 6):
            x_wait(c, k)
            x_start(c, k + 2)

    def b5(c):
        x_wait(c, 7)
        x_wait(c, 8)
        x_start(c, 9)

    def r_move(c, s, k):
        first, second = scatter[s]
        fs, gs = at[first], at[second]
        d = 1 if k % 2 == 0 else -1
        if k < 2:
            part = pl.ds(0, CUT) if k == 0 else pl.ds(CUT, group - CUT)
            return w1.at[s, c % SLOTS, fs[2], part], ro1.at[s, c, part], peer[first, d]
        if k < 4:
            return w1.at[s, c % SLOTS, fs[d]], rn1.at[s, c, k - 2], peer[first, d]
        if k < 6:
            part = pl.ds((k - 4) * (WINDOW // 2), WINDOW // 2)
            return w2.at[s, c, gs[2], part], ro2.at[s, c, part], peer[second, d]
        return w2.at[s, c, gs[d]], rn2.at[s, c, k - 6], peer[second, d]

    def r_start(c, s, k):
        src, dst, to = r_move(c, s, k)
        copy(c, RS_KIND + s * 8 + k, src, dst, to).start()

    def r_wait(c, s, k):
        arrived(c, RS_KIND + s * 8 + k, r_move(c, s, k)[1])

    def m2(c):
        x_wait(c, 9)

        turned[...] = sg[c % SLOTS].T

        for g in range(2):
            both = jnp.dot(v[2 * g * group : 2 * (g + 1) * group, :], turned[...], preferred_element_type=F32)
            for q in (2 * g, 2 * g + 1):
                part = both[(q - 2 * g) * group : (q - 2 * g + 1) * group]
                w1[0, c % SLOTS, q] = part[:, :128].astype(BF16)
                for p in range(4):
                    wq[p, q * final : (q + 1) * final] = part[p * final : (p + 1) * final, 128:]
        for p in range(4):
            w1[1, c % SLOTS, p] = wq[p].astype(BF16)
        for s in range(2):
            r_start(c, s, 0)
            r_start(c, s, 1)

    def r1(c):
        for s in range(2):
            up, down = at[scatter[s][0]][1], at[scatter[s][0]][-1]
            r_wait(c, s, 0)
            w1[s, c % SLOTS, up, :CUT] = (w1[s, c % SLOTS, up, :CUT].astype(F32) + ro1[s, c, :CUT].astype(F32)).astype(BF16)
            r_start(c, s, 2)
            r_wait(c, s, 1)
            w1[s, c % SLOTS, down, CUT:] = (w1[s, c % SLOTS, down, CUT:].astype(F32) + ro1[s, c, CUT:].astype(F32)).astype(BF16)
            r_start(c, s, 3)

    def r2(c):
        for s in range(2):
            f = at[scatter[s][0]][0]
            r_wait(c, s, 2)
            r_wait(c, s, 3)
            total = w1[s, c % SLOTS, f].astype(F32) + rn1[s, c, 0].astype(F32) + rn1[s, c, 1].astype(F32)
            total = total.astype(BF16)
            for p in range(4):
                w2[s, c, p] = total[p * STRIDE : p * STRIDE + WINDOW]
            r_start(c, s, 4)
            r_start(c, s, 5)

    def r3(c):
        h = WINDOW // 2
        for s in range(2):
            up, down = at[scatter[s][1]][1], at[scatter[s][1]][-1]
            r_wait(c, s, 4)
            w2[s, c, up, :h] = (w2[s, c, up, :h].astype(F32) + ro2[s, c, :h].astype(F32)).astype(BF16)
            r_start(c, s, 6)
            r_wait(c, s, 5)
            w2[s, c, down, h:] = (w2[s, c, down, h:].astype(F32) + ro2[s, c, h:].astype(F32)).astype(BF16)
            r_start(c, s, 7)

    def r4(c):
        sums = []
        for s in range(2):
            g = at[scatter[s][1]][0]
            r_wait(c, s, 6)
            r_wait(c, s, 7)
            total = w2[s, c, g].astype(F32) + rn2[s, c, 0].astype(F32) + rn2[s, c, 1].astype(F32)
            sums.append(pltpu.roll(total, lax.rem(WINDOW - 4 * g, WINDOW), 0))
        total = jnp.concatenate(sums, axis=1)
        total = jnp.concatenate([total, jnp.zeros((256 - WINDOW, 256), F32)], axis=0)
        gap = rc[:, c].reshape(256, 128)
        gap = jnp.concatenate([gap, gap], axis=1) + cf[0:1, :]
        out[:, c] = (total.T / gap).astype(BF16).reshape(16, BLOCK, 256)

    def rw(c):
        for s in range(2):
            for k in range(4):
                sent(c, RS_KIND + s * 8 + k, r_move(c, s, k)[0])

    def gw(c):
        for k in range(5, 10):
            sent(c, X_KIND + k, x_send(c, k)[0])

    def cw(c):
        for k in range(5):
            sent(c, X_KIND + k, x_send(c, k)[0])

    def sw(c):
        @pl.when(c == 0)
        def _():
            for k in range(7):
                t_copy(k, t_send(k)[0], peer["core"]).wait_send()

        for s in range(2):
            for k in range(7):
                sent(c, s * 7 + k, a_send(c, s, k)[0])
            for k in range(4, 8):
                sent(c, RS_KIND + s * 8 + k, r_move(c, s, k)[0])

    part = (width // 3 + 127) // 128 * 128

    def load(i):
        rows = pl.ds(i * part, min(part, width - i * part))
        return pltpu.make_async_copy(vt_hbm.at[rows], vt.at[rows], lsem.at[i])

    def tv(c):
        def turn(i, carry):
            tile = pl.ds(pl.multiple_of(i * TILE, TILE), TILE)
            v[:, tile] = vt[tile, :].T
            ends = vt[tile, main:]
            vtail[tile, :] = jnp.concatenate([ends, ends], axis=1)
            return carry

        for i in range(3):

            @pl.when(c == i)
            def _():
                load(i).wait()
                end = min((i + 1) * part, width)
                lax.fori_loop(i * part // TILE, end // TILE, turn, 0)
                if end % TILE:
                    start = end // TILE * TILE
                    v[:, start:] = vt[start:, :].T
                    ends = vt[start:, main:]
                    vtail[start:, :] = jnp.concatenate([ends, ends], axis=1)

    for i in range(3):
        load(i).start()
    for k in range(0, chunks, 2):
        pair = [a_ref[i * BLOCK : (i + 1) * BLOCK, main:] for i in (k, k + 1) if i < chunks]
        if len(pair) == 1:
            pair.append(jnp.zeros_like(pair[0]))
        tg[z, y, k // 2 * BLOCK : (k // 2 + 1) * BLOCK, :] = jnp.concatenate(pair, axis=1)

    def gp(c):
        inner, outer = col * width, (row * 16 + col) * final
        inner_row = inner // 128
        outer_row = jnp.minimum(outer // 128, col_ref.shape[0] - 3)
        for k in range(12):
            near[:, 128 * k : 128 * (k + 1)] = col_ref[pl.ds(inner_row + k, 1), :]
        for k in range(3):
            near[:, 1536 + 128 * k : 1664 + 128 * k] = col_ref[pl.ds(outer_row + k, 1), :]
        cg[...] = pltpu.roll(jnp.broadcast_to(near[:, :1536], (8, 1536)), (1536 - (inner - inner_row * 128)) % 1536, 1)
        shifted = pltpu.roll(jnp.broadcast_to(near[:, 1536:], (8, 384)), (384 - (outer - outer_row * 128)) % 384, 1)
        cf[...] = shifted[:, :256]
        flat = rc.reshape(16 * chunks * BLOCK, 128)
        for k in range(row_ref.shape[0]):
            flat[k * 128 : (k + 1) * 128, :] = jnp.broadcast_to(row_ref[k : k + 1, :], (128, 128)).T

    pl.semaphore_wait(barrier, len(peer))

    ops = dict(tv=tv, cw=cw, gw=gw, rw=rw, gp=gp, a0=a0, a1=a1, a2=a2, a3=a3, m1=m1, b1=b1, b2=b2, b3=b3, b4=b4, b5=b5, m2=m2, r1=r1, r2=r2, r3=r3, r4=r4, sw=sw)

    def step(t, carry):
        for name, late in PLAN:
            c = t - late
            pl.when(jnp.logical_and(c >= 0, c < {"tv": 3, "gp": 1}.get(name, chunks)))(functools.partial(ops[name], c))
        return carry

    lax.fori_loop(0, chunks + max(late for _, late in PLAN), step, 0)
    for k in range(chunks):
        lanes = pl.ds(k * 256, 256)
        rows = out.reshape(16 * chunks * BLOCK, 256)[lanes, :]
        o_ref[:, lanes] = rows.T[:final]


def on_device(amplitudes, integrals, row_gap, col_gap):
    rows, depth = amplitudes.shape
    width = integrals.shape[1]
    chunks = rows // BLOCK
    final = depth // 16

    vm = pl.BlockSpec(memory_space=pltpu.VMEM)
    anywhere = pl.BlockSpec(memory_space=pl.ANY)
    updated = pl.pallas_call(
        kernel,
        out_shape=jax.ShapeDtypeStruct((final, 16 * rows), BF16),
        in_specs=[vm, anywhere, vm, vm],
        out_specs=vm,
        scratch_shapes=[
            pltpu.VMEM((1, 1920), F32),
            pltpu.VMEM((8, 1536), F32),
            pltpu.VMEM((8, 256), F32),
            pltpu.VMEM((16, chunks, BLOCK, 128), F32),
            pltpu.VMEM((depth, width), BF16),
            pltpu.VMEM((width, depth), BF16),
            pltpu.VMEM((width, 128), BF16),
            pltpu.VMEM((width, 256), BF16),
            pltpu.VMEM((chunks, 4, 4, BLOCK, depth // 128 * 128), BF16),
            pltpu.VMEM((4, 4, (chunks + 1) // 2 * BLOCK, 128), BF16),
            pltpu.VMEM((SLOTS, 256, width), BF16),
            pltpu.VMEM((SLOTS, 128, width), BF16),
            pltpu.VMEM((chunks, 32, width), BF16),
            pltpu.VMEM((chunks, 2, 32, width), BF16),
            pltpu.VMEM((SLOTS, 256, width), BF16),
            pltpu.VMEM((4, depth // 4, 128), F32),
            pltpu.VMEM((2, SLOTS, 4, depth // 4, 128), BF16),
            pltpu.VMEM((2, chunks, 4, WINDOW, 128), BF16),
            pltpu.VMEM((2, chunks, depth // 4, 128), BF16),
            pltpu.VMEM((2, chunks, 2, depth // 4, 128), BF16),
            pltpu.VMEM((2, chunks, WINDOW, 128), BF16),
            pltpu.VMEM((2, chunks, 2, WINDOW, 128), BF16),
            pltpu.VMEM((16, chunks, BLOCK, 256), BF16),
            pltpu.SemaphoreType.DMA((3,)),
            pltpu.SemaphoreType.DMA((7,)),
            pltpu.SemaphoreType.DMA((7,)),
            pltpu.SemaphoreType.DMA((chunks, KINDS)),
            pltpu.SemaphoreType.DMA((chunks, KINDS)),
        ],
        compiler_params=pltpu.CompilerParams(
            collective_id=0, has_side_effects=True, vmem_limit_bytes=62 * 1024 * 1024
        ),
        cost_estimate=pl.CostEstimate(
            flops=4 * 16 * rows * depth * width, bytes_accessed=2 * depth * width, transcendentals=0
        ),
    )(amplitudes, integrals.T, row_gap.reshape(-1, 128), col_gap.reshape(-1, 128))
    return updated.T


def solution(mesh):
    return jax.shard_map(
        on_device,
        mesh=mesh,
        in_specs=(P("col", "row"), P("row", "col"), P(), P()),
        out_specs=P(None, ("row", "col")),
        check_vma=False,
    )
```

profile of v0, /device:TPU:0, one launch (start us, length us, event | category | flops | bytes accessed | tf_op | source)
XLA Modules:
  0.0 136.7 jit_solution(13125070927860820893)
XLA Ops:
  0.0 134.7 %shard_map.46 = bf16[180,1792]{1,0:T(8,128)(2,1)} custom-call(bf16[112,2880]{1,0:T(8,128)(2,1)} %a_ref.1, bf16[1440,2880]{1,0:T(8,128)(2,1)} %bitcast.5, f32[14,128]{1,0:T(8,128)} %bitcast.7, f32[180,128]{1,0:T(8,128)} %bitcast.6), custom_call_target="tpu_custom_call" | custom-call | flops 29727129600 | bytes 8294400 | tf_op jit(solution)/shard_map/pallas_call | solution.py:488
  134.7 2.0 %copy.6 = bf16[1792,180]{0,1:T(8,128)(2,1)} copy(bf16[1792,180]{0,1:T(8,128)(2,1)} %bitcast.4) | data formatting | bytes 1290240
where the time goes:
time: 137 us
  Pallas kernels  135 us (99%)
  local copies, waits for them, and re-layouts  1.97 us (1%)
    pallas_call x1, Pallas kernels, on_device(): pl.pallas_call(kernel, out_shape=jax.ShapeDtypeStruct((final, 16 * rows),...  135 us

commit v1 on v0

--- a/solution.py
+++ b/solution.py
@@ -15,6 +15,7 @@
 WINDOW = 192
 STRIDE = 176
 TILE = 128
+SHARE = 1280
 CUT = 368
 SLOTS = 4
 X_KIND = 14
@@ -75,7 +76,7 @@
     }
     strips = {step: half + index * 32 for step, index in xs.items()}
     main = ag.shape[-1]
-    gather = (("y", "z", pl.ds(0, main // 2)), ("z", "y", pl.ds(main // 2, main // 2)))
+    gather = (("y", "z", pl.ds(0, SHARE)), ("z", "y", pl.ds(SHARE, main - SHARE)))
     scatter = (("z", "y"), ("y", "z"))
 
     barrier = pltpu.get_barrier_semaphore()
@@ -135,22 +136,22 @@
         arrived(c, s * 7 + k, a_land(c, s, k))
 
     def t_line(step, start=0, size=4):
-        return tg.at[zs[step], pl.ds(start, size)]
+        return tg.at[pl.ds(start, size), ys[step]]
 
     def t_send(k):
         return (
-            (tg.at[z, y], peer["y", 1]),
-            (tg.at[z, y], peer["y", -1]),
-            (tg.at[z, ys[-1]], peer["y", 1]),
-            (t_line(0), peer["z", 1]),
-            (t_line(0), peer["z", -1]),
-            (t_line(-1, 0, 2), peer["z", 1]),
-            (t_line(1, 2, 2), peer["z", -1]),
+            (tg.at[z, y], peer["z", 1]),
+            (tg.at[z, y], peer["z", -1]),
+            (tg.at[zs[-1], y], peer["z", 1]),
+            (t_line(0), peer["y", 1]),
+            (t_line(0), peer["y", -1]),
+            (t_line(-1, 0, 2), peer["y", 1]),
+            (t_line(1, 2, 2), peer["y", -1]),
         )[k]
 
     def t_land(k):
         return (
-            tg.at[z, ys[-1]], tg.at[z, ys[1]], tg.at[z, ys[2]],
+            tg.at[zs[-1], y], tg.at[zs[1], y], tg.at[zs[2], y],
             t_line(-1), t_line(1), t_line(2, 0, 2), t_line(2, 2, 2),
         )[k]
 

time: 137 us -> 139 us (1.015)
  Pallas kernels: 135 us -> 137 us
    pallas_call x1, Pallas kernels: 135 us -> 137 us  [on_device(): pl.pallas_call(kernel, out_shape=jax.ShapeDtypeStruct((final, 16 * rows),...]
where the time goes in v1:
time: 139 us
  Pallas kernels  137 us (99%)
  local copies, waits for them, and re-layouts  1.97 us (1%)
    pallas_call x1, Pallas kernels, on_device(): pl.pallas_call(kernel, out_shape=jax.ShapeDtypeStruct((final, 16 * rows),...  137 us

profile of v1, /device:TPU:0, one launch (start us, length us, event | category | flops | bytes accessed | tf_op | source)
XLA Modules:
  0.0 138.8 jit_solution(12098023179883261961)
XLA Ops:
  0.0 136.8 %shard_map.46 = bf16[180,1792]{1,0:T(8,128)(2,1)} custom-call(bf16[112,2880]{1,0:T(8,128)(2,1)} %a_ref.1, bf16[1440,2880]{1,0:T(8,128)(2,1)} %bitcast.5, f32[14,128]{1,0:T(8,128)} %bitcast.7, f32[180,128]{1,0:T(8,128)} %bitcast.6), custom_call_target="tpu_custom_call" | custom-call | flops 29727129600 | bytes 8294400 | tf_op jit(solution)/shard_map/pallas_call | solution.py:489
  136.8 2.0 %copy.6 = bf16[1792,180]{0,1:T(8,128)(2,1)} copy(bf16[1792,180]{0,1:T(8,128)(2,1)} %bitcast.4) | data formatting | bytes 1290240

commit v2 on v0

--- a/solution.py
+++ b/solution.py
@@ -22,37 +22,37 @@
 KINDS = 40
 
 PLAN = (
-    ("r1", 8),
+    ("b3", 6),
+    ("cw", 8),
+    ("m1", 4),
+    ("b2", 5),
+    ("a3", 3),
+    ("a2", 2),
+    ("r1", 9),
+    ("rw", 12),
+    ("m2", 8),
+    ("b5", 7),
+    ("a1", 1),
+    ("a0", 0),
+    ("r4", 13),
+    ("sw", 13),
+    ("tv", 2),
+    ("gp", 5),
+    ("gw", 8),
+    ("b1", 4),
+    ("b4", 6),
     ("r2", 10),
-    ("a0", 0),
-    ("cw", 7),
-    ("m1", 3),
-    ("b2", 4),
-    ("b4", 5),
-    ("r3", 12),
-    ("a3", 2),
-    ("a2", 1),
-    ("r4", 14),
-    ("sw", 14),
-    ("tv", 0),
-    ("gp", 3),
-    ("a1", 0),
-    ("rw", 10),
-    ("m2", 6),
-    ("gw", 7),
-    ("b1", 3),
-    ("b3", 4),
-    ("b5", 5),
+    ("r3", 11),
 )
 
 
 def kernel(
-    a_ref, vt_hbm, row_ref, col_ref, o_ref,
-    near, cg, cf, rc, v, vt, vtail, turned, ag, tg, c1, cx, xo, xn, sg, wq, w1, w2, ro1, rn1, ro2, rn2, out, lsem, tsend, trecv, send, recv,
+    a_hbm, vt_hbm, row_ref, col_ref, o_ref,
+    a_ref, near, cg, cf, rc, v, vt, vtail, turned, ag, tg, c1, cx, xo, xn, sg, wq, w1, w2, ro1, rn1, ro2, rn2, lsem, tsend, trecv, send, recv,
 ):
     chunks = ag.shape[0]
     depth, width = a_ref.shape[1], v.shape[1]
-    group, final = depth // 4, o_ref.shape[0]
+    group, final = depth // 4, o_ref.shape[-1]
     row, col = lax.axis_index("row"), lax.axis_index("col")
     x, core = row // 2, row % 2
     z, y = col // 4, col % 4
@@ -383,7 +383,7 @@
         total = jnp.concatenate([total, jnp.zeros((256 - WINDOW, 256), F32)], axis=0)
         gap = rc[:, c].reshape(256, 128)
         gap = jnp.concatenate([gap, gap], axis=1) + cf[0:1, :]
-        out[:, c] = (total.T / gap).astype(BF16).reshape(16, BLOCK, 256)
+        o_ref[:, c] = (total.T / gap).astype(BF16)[:, :final].reshape(16, BLOCK, final)
 
     def rw(c):
         for s in range(2):
@@ -410,35 +410,31 @@
             for k in range(4, 8):
                 sent(c, RS_KIND + s * 8 + k, r_move(c, s, k)[0])
 
-    part = (width // 3 + 127) // 128 * 128
-
-    def load(i):
-        rows = pl.ds(i * part, min(part, width - i * part))
-        return pltpu.make_async_copy(vt_hbm.at[rows], vt.at[rows], lsem.at[i])
+    load = pltpu.make_async_copy(vt_hbm, vt, lsem.at[0])
+    entry = pltpu.make_async_copy(a_hbm, a_ref, lsem.at[1])
+    tiles = width // TILE
 
     def tv(c):
+        @pl.when(c == 0)
+        def _():
+            load.wait()
+            ends = vt[:, main:]
+            vtail[...] = jnp.concatenate([ends, ends], axis=1)
+
         def turn(i, carry):
             tile = pl.ds(pl.multiple_of(i * TILE, TILE), TILE)
             v[:, tile] = vt[tile, :].T
-            ends = vt[tile, main:]
-            vtail[tile, :] = jnp.concatenate([ends, ends], axis=1)
             return carry
 
-        for i in range(3):
-
-            @pl.when(c == i)
-            def _():
-                load(i).wait()
-                end = min((i + 1) * part, width)
-                lax.fori_loop(i * part // TILE, end // TILE, turn, 0)
-                if end % TILE:
-                    start = end // TILE * TILE
-                    v[:, start:] = vt[start:, :].T
-                    ends = vt[start:, main:]
-                    vtail[start:, :] = jnp.concatenate([ends, ends], axis=1)
-
-    for i in range(3):
-        load(i).start()
+        lax.fori_loop(2 * c, jnp.minimum(2 * c + 2, tiles), turn, 0)
+
+        @pl.when(c == 5)
+        def _():
+            v[:, tiles * TILE :] = vt[tiles * TILE :, :].T
+
+    entry.start()
+    load.start()
+    entry.wait()
     for k in range(0, chunks, 2):
         pair = [a_ref[i * BLOCK : (i + 1) * BLOCK, main:] for i in (k, k + 1) if i < chunks]
         if len(pair) == 1:
@@ -467,14 +463,10 @@
     def step(t, carry):
         for name, late in PLAN:
             c = t - late
-            pl.when(jnp.logical_and(c >= 0, c < {"tv": 3, "gp": 1}.get(name, chunks)))(functools.partial(ops[name], c))
+            pl.when(jnp.logical_and(c >= 0, c < {"tv": 6, "gp": 1}.get(name, chunks)))(functools.partial(ops[name], c))
         return carry
 
     lax.fori_loop(0, chunks + max(late for _, late in PLAN), step, 0)
-    for k in range(chunks):
-        lanes = pl.ds(k * 256, 256)
-        rows = out.reshape(16 * chunks * BLOCK, 256)[lanes, :]
-        o_ref[:, lanes] = rows.T[:final]
 
 
 def on_device(amplitudes, integrals, row_gap, col_gap):
@@ -487,10 +479,11 @@
     anywhere = pl.BlockSpec(memory_space=pl.ANY)
     updated = pl.pallas_call(
         kernel,
-        out_shape=jax.ShapeDtypeStruct((final, 16 * rows), BF16),
-        in_specs=[vm, anywhere, vm, vm],
+        out_shape=jax.ShapeDtypeStruct((16, chunks, BLOCK, final), BF16),
+        in_specs=[anywhere, anywhere, vm, vm],
         out_specs=vm,
         scratch_shapes=[
+            pltpu.VMEM((rows, depth), BF16),
             pltpu.VMEM((1, 1920), F32),
             pltpu.VMEM((8, 1536), F32),
             pltpu.VMEM((8, 256), F32),
@@ -513,8 +506,7 @@
             pltpu.VMEM((2, chunks, 2, depth // 4, 128), BF16),
             pltpu.VMEM((2, chunks, WINDOW, 128), BF16),
             pltpu.VMEM((2, chunks, 2, WINDOW, 128), BF16),
-            pltpu.VMEM((16, chunks, BLOCK, 256), BF16),
-            pltpu.SemaphoreType.DMA((3,)),
+            pltpu.SemaphoreType.DMA((2,)),
             pltpu.SemaphoreType.DMA((7,)),
             pltpu.SemaphoreType.DMA((7,)),
             pltpu.SemaphoreType.DMA((chunks, KINDS)),
@@ -527,7 +519,7 @@
             flops=4 * 16 * rows * depth * width, bytes_accessed=2 * depth * width, transcendentals=0
         ),
     )(amplitudes, integrals.T, row_gap.reshape(-1, 128), col_gap.reshape(-1, 128))
-    return updated.T
+    return updated.reshape(16 * rows, final)
 
 
 def solution(mesh):

time: 137 us -> 138 us (level)
    reshape x0 -> x1, local copies, waits for them, and re-layouts: none -> 2.14 us  [on_device(): return updated.reshape(16 * rows, final)]
    unnamed x1 -> x0, local copies, waits for them, and re-layouts: 1.97 us -> none
where the time goes in v2:
time: 138 us
  Pallas kernels  136 us (99%)
  local copies, waits for them, and re-layouts  2.14 us (2%)
    pallas_call x1, Pallas kernels, on_device(): pl.pallas_call(kernel, out_shape=jax.ShapeDtypeStruct((16, chunks, BLOCK,...  136 us

profile of v2, /device:TPU:0, one launch (start us, length us, event | category | flops | bytes accessed | tf_op | source)
XLA Modules:
  0.0 138.1 jit_solution(17802449463700832090)
XLA Ops:
  0.0 135.9 %shard_map.46 = bf16[16,7,16,180]{3,2,1,0:T(8,128)(2,1)} custom-call(bf16[112,2880]{1,0:T(8,128)(2,1)} %a_hbm.1, bf16[1440,2880]{1,0:T(8,128)(2,1)} %bitcast.5, f32[14,128]{1,0:T(8,128)} %bitcast.7, f32[180,128]{1,0:T(8,128)} %bitcast.6), custom_call_target="tpu_custom_call" | custom-call | flops 29727129600 | bytes 8294400 | tf_op jit(solution)/shard_map/pallas_call | solution.py:480
  135.9 2.1 %copy.5 = bf16[1792,180]{0,1:T(8,128)(2,1)} copy(bf16[1792,180]{1,0:T(8,128)(2,1)} %bitcast.4) | data formatting | bytes 1290240 | tf_op jit(solution)/shard_map/reshape | solution.py:522

commit v3 on v2

--- a/solution.py
+++ b/solution.py
@@ -48,7 +48,7 @@
 
 def kernel(
     a_hbm, vt_hbm, row_ref, col_ref, o_ref,
-    a_ref, near, cg, cf, rc, v, vt, vtail, turned, ag, tg, c1, cx, xo, xn, sg, wq, w1, w2, ro1, rn1, ro2, rn2, lsem, tsend, trecv, send, recv,
+    a_ref, near, cg, cf, rc, v, vt, vtail, turned, ag, tg, c1, cx, xo, xn, sg, wq, w1, w2, ro1, rn1, ro2, rn2, pace, lsem, tsend, trecv, send, recv,
 ):
     chunks = ag.shape[0]
     depth, width = a_ref.shape[1], v.shape[1]
@@ -339,6 +339,8 @@
             r_start(c, s, 1)
 
     def r1(c):
+        pl.semaphore_signal(pace.at[c], inc=1, device_id=peer["core"], device_id_type=MESH)
+        pl.semaphore_wait(pace.at[c], 1)
         for s in range(2):
             up, down = at[scatter[s][0]][1], at[scatter[s][0]][-1]
             r_wait(c, s, 0)
@@ -506,6 +508,7 @@
             pltpu.VMEM((2, chunks, 2, depth // 4, 128), BF16),
             pltpu.VMEM((2, chunks, WINDOW, 128), BF16),
             pltpu.VMEM((2, chunks, 2, WINDOW, 128), BF16),
+            pltpu.SemaphoreType.REGULAR((chunks,)),
             pltpu.SemaphoreType.DMA((2,)),
             pltpu.SemaphoreType.DMA((7,)),
             pltpu.SemaphoreType.DMA((7,)),

time: 138 us -> 139 us (level)
  no operation moved by 1% of the time
where the time goes in v3:
time: 139 us
  Pallas kernels  137 us (99%)
  local copies, waits for them, and re-layouts  2.14 us (2%)
    pallas_call x1, Pallas kernels, on_device(): pl.pallas_call(kernel, out_shape=jax.ShapeDtypeStruct((16, chunks, BLOCK,...  137 us

profile of v3, /device:TPU:0, one launch (start us, length us, event | category | flops | bytes accessed | tf_op | source)
XLA Modules:
  0.0 139.1 jit_solution(1130059529898755601)
XLA Ops:
  0.0 137.0 %shard_map.46 = bf16[16,7,16,180]{3,2,1,0:T(8,128)(2,1)} custom-call(bf16[112,2880]{1,0:T(8,128)(2,1)} %a_hbm.1, bf16[1440,2880]{1,0:T(8,128)(2,1)} %bitcast.5, f32[14,128]{1,0:T(8,128)} %bitcast.7, f32[180,128]{1,0:T(8,128)} %bitcast.6), custom_call_target="tpu_custom_call" | custom-call | flops 29727129600 | bytes 8294400 | tf_op jit(solution)/shard_map/pallas_call | solution.py:482
  137.0 2.1 %copy.5 = bf16[1792,180]{0,1:T(8,128)(2,1)} copy(bf16[1792,180]{1,0:T(8,128)(2,1)} %bitcast.4) | data formatting | bytes 1290240 | tf_op jit(solution)/shard_map/reshape | solution.py:525

commit v4 on v2

--- a/solution.py
+++ b/solution.py
@@ -22,27 +22,27 @@
 KINDS = 40
 
 PLAN = (
-    ("b3", 6),
-    ("cw", 8),
-    ("m1", 4),
-    ("b2", 5),
-    ("a3", 3),
-    ("a2", 2),
-    ("r1", 9),
-    ("rw", 12),
-    ("m2", 8),
-    ("b5", 7),
-    ("a1", 1),
+    ("r1", 8),
+    ("r2", 10),
     ("a0", 0),
-    ("r4", 13),
-    ("sw", 13),
-    ("tv", 2),
-    ("gp", 5),
-    ("gw", 8),
-    ("b1", 4),
-    ("b4", 6),
-    ("r2", 10),
-    ("r3", 11),
+    ("cw", 7),
+    ("m1", 3),
+    ("b2", 4),
+    ("b4", 5),
+    ("r3", 12),
+    ("a3", 2),
+    ("a2", 1),
+    ("r4", 14),
+    ("sw", 14),
+    ("a1", 0),
+    ("tv", 0),
+    ("gp", 3),
+    ("rw", 10),
+    ("m2", 6),
+    ("gw", 7),
+    ("b1", 3),
+    ("b3", 4),
+    ("b5", 5),
 )
 
 
@@ -71,6 +71,8 @@
         ("y", -1): (row, z * 4 + ys[-1]),
         ("z", 1): (row, zs[1] * 4 + y),
         ("z", -1): (row, zs[-1] * 4 + y),
+        ("y", 2): (row, z * 4 + ys[2]),
+        ("z", 2): (row, zs[2] * 4 + y),
         "core": (x * 2 + 1 - core, col),
     }
     strips = {step: half + index * 32 for step, index in xs.items()}
@@ -141,7 +143,7 @@
         return (
             (tg.at[z, y], peer["y", 1]),
             (tg.at[z, y], peer["y", -1]),
-            (tg.at[z, ys[-1]], peer["y", 1]),
+            (tg.at[z, y], peer["y", 2]),
             (t_line(0), peer["z", 1]),
             (t_line(0), peer["z", -1]),
             (t_line(-1, 0, 2), peer["z", 1]),
@@ -172,7 +174,12 @@
         for s in range(2):
             a_start(c, s, 0)
             a_start(c, s, 1)
-        pl.when(c == 0)(lambda: t_start(0, 1))
+
+        @pl.when(c == 0)
+        def _():
+            for s in range(2):
+                copy(c, s * 7 + 2, block(s, c, 0), block(s, c, 0), peer[gather[s][0], 2]).start()
+            t_start(0, 1, 2)
 
     def a1(c):
         def forward(d):
@@ -182,10 +189,10 @@
 
         @pl.when(c == 0)
         def _():
-            t_wait(0)
-            t_start(2)
-
-        pl.when(c % 2 == 0)(lambda: forward(1))
+            for s in range(2):
+                a_wait(c, s, 0)
+
+        pl.when(jnp.logical_and(c % 2 == 0, c > 0))(lambda: forward(1))
         pl.when(c % 2 == 1)(lambda: forward(-1))
 
     def a2(c):
@@ -198,7 +205,7 @@
 
         @pl.when(c == 0)
         def _():
-            t_wait(1, 2)
+            t_wait(0, 1, 2)
             t_start(3, 4)
 
     def a3(c):
@@ -305,9 +312,9 @@
         d = 1 if k % 2 == 0 else -1
         if k < 2:
             part = pl.ds(0, CUT) if k == 0 else pl.ds(CUT, group - CUT)
-            return w1.at[s, c % SLOTS, fs[2], part], ro1.at[s, c, part], peer[first, d]
+            return w1.at[s, c % SLOTS, fs[2], part], ro1.at[s, c % SLOTS, part], peer[first, d]
         if k < 4:
-            return w1.at[s, c % SLOTS, fs[d]], rn1.at[s, c, k - 2], peer[first, d]
+            return w1.at[s, c % SLOTS, fs[d]], rn1.at[s, c % SLOTS, k - 2], peer[first, d]
         if k < 6:
             part = pl.ds((k - 4) * (WINDOW // 2), WINDOW // 2)
             return w2.at[s, c, gs[2], part], ro2.at[s, c, part], peer[second, d]
@@ -316,6 +323,10 @@
     def r_start(c, s, k):
         src, dst, to = r_move(c, s, k)
         copy(c, RS_KIND + s * 8 + k, src, dst, to).start()
+
+    def far_copy(c, s):
+        second = scatter[s][1]
+        return copy(c, RS_KIND + s * 8 + 4, w2.at[s, c, at[second][2]], ro2.at[s, c], peer[second, 2])
 
     def r_wait(c, s, k):
         arrived(c, RS_KIND + s * 8 + k, r_move(c, s, k)[1])
@@ -339,37 +350,52 @@
             r_start(c, s, 1)
 
     def r1(c):
+        o = c % SLOTS
+        for s in range(2):
+            r_wait(c, s, 0)
+            r_wait(c, s, 1)
         for s in range(2):
             up, down = at[scatter[s][0]][1], at[scatter[s][0]][-1]
-            r_wait(c, s, 0)
-            w1[s, c % SLOTS, up, :CUT] = (w1[s, c % SLOTS, up, :CUT].astype(F32) + ro1[s, c, :CUT].astype(F32)).astype(BF16)
+            w1[s, o, up, :CUT] = (w1[s, o, up, :CUT].astype(F32) + ro1[s, o, :CUT].astype(F32)).astype(BF16)
             r_start(c, s, 2)
-            r_wait(c, s, 1)
-            w1[s, c % SLOTS, down, CUT:] = (w1[s, c % SLOTS, down, CUT:].astype(F32) + ro1[s, c, CUT:].astype(F32)).astype(BF16)
+            w1[s, o, down, CUT:] = (w1[s, o, down, CUT:].astype(F32) + ro1[s, o, CUT:].astype(F32)).astype(BF16)
             r_start(c, s, 3)
 
     def r2(c):
+        o = c % SLOTS
         for s in range(2):
             f = at[scatter[s][0]][0]
             r_wait(c, s, 2)
             r_wait(c, s, 3)
-            total = w1[s, c % SLOTS, f].astype(F32) + rn1[s, c, 0].astype(F32) + rn1[s, c, 1].astype(F32)
+            total = w1[s, o, f].astype(F32) + rn1[s, o, 0].astype(F32) + rn1[s, o, 1].astype(F32)
             total = total.astype(BF16)
             for p in range(4):
                 w2[s, c, p] = total[p * STRIDE : p * STRIDE + WINDOW]
-            r_start(c, s, 4)
-            r_start(c, s, 5)
+
+            @pl.when(c < chunks - 1)
+            def _():
+                r_start(c, s, 4)
+                r_start(c, s, 5)
+
+            @pl.when(c == chunks - 1)
+            def _():
+                far_copy(c, s).start()
+                r_start(c, s, 6)
+                r_start(c, s, 7)
 
     def r3(c):
         h = WINDOW // 2
-        for s in range(2):
-            up, down = at[scatter[s][1]][1], at[scatter[s][1]][-1]
-            r_wait(c, s, 4)
-            w2[s, c, up, :h] = (w2[s, c, up, :h].astype(F32) + ro2[s, c, :h].astype(F32)).astype(BF16)
-            r_start(c, s, 6)
-            r_wait(c, s, 5)
-            w2[s, c, down, h:] = (w2[s, c, down, h:].astype(F32) + ro2[s, c, h:].astype(F32)).astype(BF16)
-            r_start(c, s, 7)
+
+        @pl.when(c < chunks - 1)
+        def _():
+            for s in range(2):
+                up, down = at[scatter[s][1]][1], at[scatter[s][1]][-1]
+                r_wait(c, s, 4)
+                w2[s, c, up, :h] = (w2[s, c, up, :h].astype(F32) + ro2[s, c, :h].astype(F32)).astype(BF16)
+                r_start(c, s, 6)
+                r_wait(c, s, 5)
+                w2[s, c, down, h:] = (w2[s, c, down, h:].astype(F32) + ro2[s, c, h:].astype(F32)).astype(BF16)
+                r_start(c, s, 7)
 
     def r4(c):
         sums = []
@@ -377,7 +403,9 @@
             g = at[scatter[s][1]][0]
             r_wait(c, s, 6)
             r_wait(c, s, 7)
+            pl.when(c == chunks - 1)(lambda: far_copy(c, s).wait_recv())
             total = w2[s, c, g].astype(F32) + rn2[s, c, 0].astype(F32) + rn2[s, c, 1].astype(F32)
+            total = total + jnp.where(c == chunks - 1, ro2[s, c].astype(F32), 0.0)
             sums.append(pltpu.roll(total, lax.rem(WINDOW - 4 * g, WINDOW), 0))
         total = jnp.concatenate(sums, axis=1)
         total = jnp.concatenate([total, jnp.zeros((256 - WINDOW, 256), F32)], axis=0)
@@ -407,8 +435,16 @@
         for s in range(2):
             for k in range(7):
                 sent(c, s * 7 + k, a_send(c, s, k)[0])
-            for k in range(4, 8):
+            for k in (6, 7):
                 sent(c, RS_KIND + s * 8 + k, r_move(c, s, k)[0])
+
+            @pl.when(c < chunks - 1)
+            def _():
+                for k in (4, 5):
+                    sent(c, RS_KIND + s * 8 + k, r_move(c, s, k)[0])
+
+            pl.when(c == chunks - 1)(lambda: far_copy(c, s).wait_send())
+
 
     load = pltpu.make_async_copy(vt_hbm, vt, lsem.at[0])
     entry = pltpu.make_async_copy(a_hbm, a_ref, lsem.at[1])
@@ -502,8 +538,8 @@
             pltpu.VMEM((4, depth // 4, 128), F32),
             pltpu.VMEM((2, SLOTS, 4, depth // 4, 128), BF16),
             pltpu.VMEM((2, chunks, 4, WINDOW, 128), BF16),
-            pltpu.VMEM((2, chunks, depth // 4, 128), BF16),
-            pltpu.VMEM((2, chunks, 2, depth // 4, 128), BF16),
+            pltpu.VMEM((2, SLOTS, depth // 4, 128), BF16),
+            pltpu.VMEM((2, SLOTS, 2, depth // 4, 128), BF16),
             pltpu.VMEM((2, chunks, WINDOW, 128), BF16),
             pltpu.VMEM((2, chunks, 2, WINDOW, 128), BF16),
             pltpu.SemaphoreType.DMA((2,)),

time: 138 us -> 137 us (level)
  Pallas kernels: 136 us -> 134 us
    pallas_call x1, Pallas kernels: 136 us -> 134 us  [on_device(): pl.pallas_call(kernel, out_shape=jax.ShapeDtypeStruct((16, chunks, BLOCK,...]
where the time goes in v4:
time: 137 us; the launch traced here: 136 us
  Pallas kernels  134 us (98%)
  local copies, waits for them, and re-layouts  2.14 us (2%)
    pallas_call x1, Pallas kernels, on_device(): pl.pallas_call(kernel, out_shape=jax.ShapeDtypeStruct((16, chunks, BLOCK,...  134 us

profile of v4, /device:TPU:0, one launch (start us, length us, event | category | flops | bytes accessed | tf_op | source)
XLA Modules:
  0.0 136.4 jit_solution(1775986637978905618)
XLA Ops:
  0.0 134.2 %shard_map.46 = bf16[16,7,16,180]{3,2,1,0:T(8,128)(2,1)} custom-call(bf16[112,2880]{1,0:T(8,128)(2,1)} %a_hbm.1, bf16[1440,2880]{1,0:T(8,128)(2,1)} %bitcast.5, f32[14,128]{1,0:T(8,128)} %bitcast.7, f32[180,128]{1,0:T(8,128)} %bitcast.6), custom_call_target="tpu_custom_call" | custom-call | flops 29727129600 | bytes 8294400 | tf_op jit(solution)/shard_map/pallas_call | solution.py:516
  134.2 2.1 %copy.5 = bf16[1792,180]{0,1:T(8,128)(2,1)} copy(bf16[1792,180]{1,0:T(8,128)(2,1)} %bitcast.4) | data formatting | bytes 1290240 | tf_op jit(solution)/shard_map/reshape | solution.py:558

commit v5 on v4

--- a/solution.py
+++ b/solution.py
@@ -26,6 +26,7 @@
     ("r2", 10),
     ("a0", 0),
     ("cw", 7),
+    ("aw", 7),
     ("m1", 3),
     ("b2", 4),
     ("b4", 5),
@@ -230,12 +231,12 @@
         ends = tg[:, :, pl.ds(pl.multiple_of(c // 2 * BLOCK, BLOCK), BLOCK), :].reshape(16 * BLOCK, 128)
         mine = lax.broadcasted_iota(jnp.int32, (16 * BLOCK, 128), 1) // 64 == c % 2
         ends = jnp.where(mine, ends.astype(F32), 0.0).astype(BF16)
-        rows = ag[c].reshape(16 * BLOCK, main)
+        rows = jnp.concatenate([ag[c].reshape(16 * BLOCK, main), ends], axis=1)
         middle = (width // 2 + 127) // 128 * 128
         last = (((1,), (1,)), ((), ()))
         for lo, hi in ((0, middle), (middle, width)):
-            part = lax.dot_general(vt[lo:hi, :main], rows, last, preferred_element_type=F32)
-            part = part + lax.dot_general(vtail[lo:hi], ends, last, preferred_element_type=F32)
+            left = jnp.concatenate([vt[lo:hi, :main], vtail[lo:hi]], axis=1)
+            part = lax.dot_general(left, rows, last, preferred_element_type=F32)
             c1[c % SLOTS, :, lo:hi] = part.astype(BF16).T
         x_start(c, 0)
 
@@ -275,7 +276,7 @@
     def b1(c):
         x_wait(c, 0)
         rows = pl.ds(pl.multiple_of(half, 128), 128)
-        c1[c % SLOTS, rows, :] = (c1[c % SLOTS, rows, :].astype(F32) + cx[c % SLOTS].astype(F32)).astype(BF16)
+        c1[c % SLOTS, rows, :] = c1[c % SLOTS, rows, :] + cx[c % SLOTS]
         x_start(c, 1)
         x_start(c, 2)
 
@@ -283,7 +284,7 @@
         for k, step in ((1, 1), (2, -1)):
             x_wait(c, k)
             part, rows = pl.ds(16 * (k - 1), 16), piece(step, 16 * (k - 1), 16)
-            c1[c % SLOTS, rows, :] = (c1[c % SLOTS, rows, :].astype(F32) + xo[c, part].astype(F32)).astype(BF16)
+            c1[c % SLOTS, rows, :] = c1[c % SLOTS, rows, :] + xo[c, part]
             x_start(c, k + 2)
 
     def b3(c):
@@ -356,9 +357,9 @@
             r_wait(c, s, 1)
         for s in range(2):
             up, down = at[scatter[s][0]][1], at[scatter[s][0]][-1]
-            w1[s, o, up, :CUT] = (w1[s, o, up, :CUT].astype(F32) + ro1[s, o, :CUT].astype(F32)).astype(BF16)
+            w1[s, o, up, :CUT] = w1[s, o, up, :CUT] + ro1[s, o, :CUT]
             r_start(c, s, 2)
-            w1[s, o, down, CUT:] = (w1[s, o, down, CUT:].astype(F32) + ro1[s, o, CUT:].astype(F32)).astype(BF16)
+            w1[s, o, down, CUT:] = w1[s, o, down, CUT:] + ro1[s, o, CUT:]
             r_start(c, s, 3)
 
     def r2(c):
@@ -391,10 +392,10 @@
             for s in range(2):
                 up, down = at[scatter[s][1]][1], at[scatter[s][1]][-1]
                 r_wait(c, s, 4)
-                w2[s, c, up, :h] = (w2[s, c, up, :h].astype(F32) + ro2[s, c, :h].astype(F32)).astype(BF16)
+                w2[s, c, up, :h] = w2[s, c, up, :h] + ro2[s, c, :h]
                 r_start(c, s, 6)
                 r_wait(c, s, 5)
-                w2[s, c, down, h:] = (w2[s, c, down, h:].astype(F32) + ro2[s, c, h:].astype(F32)).astype(BF16)
+                w2[s, c, down, h:] = w2[s, c, down, h:] + ro2[s, c, h:]
                 r_start(c, s, 7)
 
     def r4(c):
@@ -426,7 +427,7 @@
         for k in range(5):
             sent(c, X_KIND + k, x_send(c, k)[0])
 
-    def sw(c):
+    def aw(c):
         @pl.when(c == 0)
         def _():
             for k in range(7):
@@ -435,6 +436,9 @@
         for s in range(2):
             for k in range(7):
                 sent(c, s * 7 + k, a_send(c, s, k)[0])
+
+    def sw(c):
+        for s in range(2):
             for k in (6, 7):
                 sent(c, RS_KIND + s * 8 + k, r_move(c, s, k)[0])
 
@@ -444,7 +448,6 @@
                     sent(c, RS_KIND + s * 8 + k, r_move(c, s, k)[0])
 
             pl.when(c == chunks - 1)(lambda: far_copy(c, s).wait_send())
-
 
     load = pltpu.make_async_copy(vt_hbm, vt, lsem.at[0])
     entry = pltpu.make_async_copy(a_hbm, a_ref, lsem.at[1])
@@ -494,7 +497,7 @@
 
     pl.semaphore_wait(barrier, len(peer))
 
-    ops = dict(tv=tv, cw=cw, gw=gw, rw=rw, gp=gp, a0=a0, a1=a1, a2=a2, a3=a3, m1=m1, b1=b1, b2=b2, b3=b3, b4=b4, b5=b5, m2=m2, r1=r1, r2=r2, r3=r3, r4=r4, sw=sw)
+    ops = dict(tv=tv, aw=aw, cw=cw, gw=gw, rw=rw, gp=gp, a0=a0, a1=a1, a2=a2, a3=a3, m1=m1, b1=b1, b2=b2, b3=b3, b4=b4, b5=b5, m2=m2, r1=r1, r2=r2, r3=r3, r4=r4, sw=sw)
 
     def step(t, carry):
         for name, late in PLAN:

time: 137 us -> 137 us (level)
  no operation moved by 1% of the time
where the time goes in v5:
time: 137 us; the launch traced here: 136 us
  Pallas kernels  134 us (98%)
  local copies, waits for them, and re-layouts  2.14 us (2%)
    pallas_call x1, Pallas kernels, on_device(): pl.pallas_call(kernel, out_shape=jax.ShapeDtypeStruct((16, chunks, BLOCK,...  134 us

profile of v5, /device:TPU:0, one launch (start us, length us, event | category | flops | bytes accessed | tf_op | source)
XLA Modules:
  0.0 136.3 jit_solution(10292111918073389508)
XLA Ops:
  0.0 134.2 %shard_map.46 = bf16[16,7,16,180]{3,2,1,0:T(8,128)(2,1)} custom-call(bf16[112,2880]{1,0:T(8,128)(2,1)} %a_hbm.1, bf16[1440,2880]{1,0:T(8,128)(2,1)} %bitcast.5, f32[14,128]{1,0:T(8,128)} %bitcast.7, f32[180,128]{1,0:T(8,128)} %bitcast.6), custom_call_target="tpu_custom_call" | custom-call | flops 29727129600 | bytes 8294400 | tf_op jit(solution)/shard_map/pallas_call | solution.py:519
  134.2 2.1 %copy.5 = bf16[1792,180]{0,1:T(8,128)(2,1)} copy(bf16[1792,180]{1,0:T(8,128)(2,1)} %bitcast.4) | data formatting | bytes 1290240 | tf_op jit(solution)/shard_map/reshape | solution.py:561

commit v6 on v5

--- a/solution.py
+++ b/solution.py
@@ -36,7 +36,7 @@
     ("r4", 14),
     ("sw", 14),
     ("a1", 0),
-    ("tv", 0),
+    ("tv", 1),
     ("gp", 3),
     ("rw", 10),
     ("m2", 6),

time: 137 us -> 136 us (level)
  no operation moved by 1% of the time
where the time goes in v6:
time: 136 us
  Pallas kernels  134 us (99%)
  local copies, waits for them, and re-layouts  2.14 us (2%)
    pallas_call x1, Pallas kernels, on_device(): pl.pallas_call(kernel, out_shape=jax.ShapeDtypeStruct((16, chunks, BLOCK,...  134 us

profile of v6, /device:TPU:0, one launch (start us, length us, event | category | flops | bytes accessed | tf_op | source)
XLA Modules:
  0.0 135.8 jit_solution(6329104694620398616)
XLA Ops:
  0.0 133.7 %shard_map.46 = bf16[16,7,16,180]{3,2,1,0:T(8,128)(2,1)} custom-call(bf16[112,2880]{1,0:T(8,128)(2,1)} %a_hbm.1, bf16[1440,2880]{1,0:T(8,128)(2,1)} %bitcast.5, f32[14,128]{1,0:T(8,128)} %bitcast.7, f32[180,128]{1,0:T(8,128)} %bitcast.6), custom_call_target="tpu_custom_call" | custom-call | flops 29727129600 | bytes 8294400 | tf_op jit(solution)/shard_map/pallas_call | solution.py:519
  133.7 2.1 %copy.5 = bf16[1792,180]{0,1:T(8,128)(2,1)} copy(bf16[1792,180]{1,0:T(8,128)(2,1)} %bitcast.4) | data formatting | bytes 1290240 | tf_op jit(solution)/shard_map/reshape | solution.py:561

commit v7 on v6

--- a/solution.py
+++ b/solution.py
@@ -25,6 +25,7 @@
     ("r1", 8),
     ("r2", 10),
     ("a0", 0),
+    ("a1", 1),
     ("cw", 7),
     ("aw", 7),
     ("m1", 3),
@@ -35,7 +36,6 @@
     ("a2", 1),
     ("r4", 14),
     ("sw", 14),
-    ("a1", 0),
     ("tv", 1),
     ("gp", 3),
     ("rw", 10),

time: 136 us -> 137 us (level)
  no operation moved by 1% of the time
where the time goes in v7:
time: 137 us
  Pallas kernels  135 us (99%)
  local copies, waits for them, and re-layouts  2.14 us (2%)
    pallas_call x1, Pallas kernels, on_device(): pl.pallas_call(kernel, out_shape=jax.ShapeDtypeStruct((16, chunks, BLOCK,...  135 us

profile of v7, /device:TPU:0, one launch (start us, length us, event | category | flops | bytes accessed | tf_op | source)
XLA Modules:
  0.0 136.8 jit_solution(670774218954684273)
XLA Ops:
  0.0 134.7 %shard_map.46 = bf16[16,7,16,180]{3,2,1,0:T(8,128)(2,1)} custom-call(bf16[112,2880]{1,0:T(8,128)(2,1)} %a_hbm.1, bf16[1440,2880]{1,0:T(8,128)(2,1)} %bitcast.5, f32[14,128]{1,0:T(8,128)} %bitcast.7, f32[180,128]{1,0:T(8,128)} %bitcast.6), custom_call_target="tpu_custom_call" | custom-call | flops 29727129600 | bytes 8294400 | tf_op jit(solution)/shard_map/pallas_call | solution.py:519
  134.7 2.1 %copy.5 = bf16[1792,180]{0,1:T(8,128)(2,1)} copy(bf16[1792,180]{1,0:T(8,128)(2,1)} %bitcast.4) | data formatting | bytes 1290240 | tf_op jit(solution)/shard_map/reshape | solution.py:561

commit v8 on v6

--- a/solution.py
+++ b/solution.py
@@ -25,6 +25,7 @@
     ("r1", 8),
     ("r2", 10),
     ("a0", 0),
+    ("a2", 1),
     ("cw", 7),
     ("aw", 7),
     ("m1", 3),
@@ -32,7 +33,6 @@
     ("b4", 5),
     ("r3", 12),
     ("a3", 2),
-    ("a2", 1),
     ("r4", 14),
     ("sw", 14),
     ("a1", 0),

time: 136 us -> 139 us (1.022)
  Pallas kernels: 134 us -> 136 us
    pallas_call x1, Pallas kernels: 134 us -> 136 us  [on_device(): pl.pallas_call(kernel, out_shape=jax.ShapeDtypeStruct((16, chunks, BLOCK,...]
where the time goes in v8:
time: 139 us
  Pallas kernels  136 us (98%)
  local copies, waits for them, and re-layouts  2.14 us (2%)
    pallas_call x1, Pallas kernels, on_device(): pl.pallas_call(kernel, out_shape=jax.ShapeDtypeStruct((16, chunks, BLOCK,...  136 us

profile of v8, /device:TPU:0, one launch (start us, length us, event | category | flops | bytes accessed | tf_op | source)
XLA Modules:
  0.0 138.6 jit_solution(12961334654768878979)
XLA Ops:
  0.0 136.5 %shard_map.46 = bf16[16,7,16,180]{3,2,1,0:T(8,128)(2,1)} custom-call(bf16[112,2880]{1,0:T(8,128)(2,1)} %a_hbm.1, bf16[1440,2880]{1,0:T(8,128)(2,1)} %bitcast.5, f32[14,128]{1,0:T(8,128)} %bitcast.7, f32[180,128]{1,0:T(8,128)} %bitcast.6), custom_call_target="tpu_custom_call" | custom-call | flops 29727129600 | bytes 8294400 | tf_op jit(solution)/shard_map/pallas_call | solution.py:519
  136.5 2.1 %copy.5 = bf16[1792,180]{0,1:T(8,128)(2,1)} copy(bf16[1792,180]{1,0:T(8,128)(2,1)} %bitcast.4) | data formatting | bytes 1290240 | tf_op jit(solution)/shard_map/reshape | solution.py:561
